TPU v7x, 32 devices: a whole 2x2x4 slice. The times are simulated.
32 devices in a mesh: seq: 16 (over z, y, x), head: 2 (over core).
Axes of the slice: x: 2, y: 2, z: 4, core: 2. Of those that a mesh axis runs over, the one named last changes fastest.
Arguments:
- probe_vectors: bfloat16 [2048, 4096], P('seq', 'head'), may hold values from -170 to 170
- mentor_address_vectors: bfloat16 [2048, 1024], P('seq', 'head'), may hold values from -7 to 7
- mentor_content_vectors: bfloat16 [2048, 1024], P('seq', 'head'), may hold values from -6 to 6
- previous_position_blend: float32 [4, 32, 128], P(None, 'head'), may hold values from 0 to 1
- feature_fading_exponent: float32 [32, 128], P('head'), may hold values from -9.5 to -2.5
- fading_narrowing_matrix: float32 [32, 128, 64], P('head'), may hold values from -0.5 to 0.5
- fading_widening_matrix: float32 [32, 64, 128], P('head'), may hold values from -0.75 to 0.75
- diagonal_extra_amount: float32 [32, 128], P('head'), may hold values from -1 to 1
Outputs:
- grad_mix: float32 [4, 32, 128], P(None, 'head')
- grad_decay: float32 [32, 128], P('head')
- grad_down: float32 [32, 128, 64], P('head')
- grad_up: float32 [32, 64, 128], P('head')
- grad_bonus: float32 [32, 128], P('head')
All inputs are finite; a program needn't handle non-finite values.
Results may differ from a plain program's by a relative error of at most 0.0035.
Values may be sent and summed in bfloat16 or wider, within the bound.
No kernel may reach another device: no remote copies, remote signals or barrier semaphores. Data moves between devices by JAX's collectives and lax.ppermute only.
A program may use at most 128 MiB of HBM per device.

v0:
```python
import math

import jax
import jax.numpy as jnp
from jax import lax
from jax.sharding import PartitionSpec as P

highest_precision = lax.Precision.HIGHEST
neg_large = -1e30
norm_eps = 0.00064


def passed_along(x, axis, by):
    devices = lax.axis_size(axis)
    pairs = [(i, i + by) for i in range(devices) if 0 <= i + by < devices]
    return lax.ppermute(x, axis, pairs)


def prefix(x, axis, combine, identity, reverse):
    devices, index = (lax.axis_size(axis), lax.axis_index(axis))
    everything = jax.tree.map(lambda part: lax.all_gather(part, axis), x)
    start = jax.tree.map(
        lambda part, zero: jnp.broadcast_to(jnp.asarray(zero, part.dtype), part.shape), x, identity
    )

    def lap(k, before):
        at = devices - 1 - k if reverse else k
        reached = at > index if reverse else at < index
        new = combine(before, jax.tree.map(lambda part: part[at], everything))
        return jax.tree.map(lambda a, b: jnp.where(reached, a, b), new, before)

    return lax.fori_loop(0, devices, lap, start)


def link_states(first_part, second_part):
    return (
        first_part[0] * second_part[0],
        second_part[0][..., None] * first_part[1] + second_part[1],
    )


def group_norm(values_in):
    centre = jnp.mean(values_in, axis=-1, keepdims=True)
    centered = values_in - centre
    spread = jnp.mean(centered * centered, axis=-1, keepdims=True)
    return centered * lax.rsqrt(spread + norm_eps)


def segment_carry_forward(diagonal_extra_vector, carried_memory, hidden_activations):
    memory_matrix, log_sofar = carried_memory
    gate_vectors, lagged_address_blend, lagged_content_blend, token_log_decay = hidden_activations
    block_len = gate_vectors.shape[0]
    inclusive = jnp.cumsum(token_log_decay, axis=0)
    exclusive = inclusive - token_log_decay
    carried_in = jnp.einsum(
        "thi,hij->thj",
        gate_vectors * jnp.exp(exclusive),
        memory_matrix,
        precision=highest_precision,
    )
    position = jnp.arange(block_len, dtype=jnp.int32)
    before = (position[:, None] > position[None, :])[:, :, None, None]
    spread = jnp.where(before, exclusive[:, None] - inclusive[None, :], 0.0)
    factor = jnp.where(before, jnp.exp(spread), 0.0)
    scores = jnp.einsum(
        "thi,shi,tshi->hts", gate_vectors, lagged_address_blend, factor, precision=highest_precision
    )
    inner_part = jnp.einsum(
        "hts,shj->thj", scores, lagged_content_blend, precision=highest_precision
    )
    diagonal_contribution = (
        jnp.sum(gate_vectors * diagonal_extra_vector * lagged_address_blend, axis=-1)[..., None]
        * lagged_content_blend
    )
    block_total = inclusive[-1]
    new_state = jnp.exp(block_total)[:, :, None] * memory_matrix + jnp.einsum(
        "shi,shj->hij",
        lagged_address_blend * jnp.exp(block_total - inclusive),
        lagged_content_blend,
        precision=highest_precision,
    )
    rate_out = gate_vectors * jnp.exp(log_sofar + exclusive)
    return (
        (new_state, log_sofar + block_total),
        (carried_in + inner_part + diagonal_contribution, rate_out),
    )


def keep_same(parts):
    return parts


def attend(
    block_rows, starts, mentor_address_vectors, mentor_content_vectors, groups, per_group, width
):
    half = block_rows.shape[0] // 2
    query_halves = block_rows.reshape(2, half, groups, per_group, width)
    query_pos = jnp.stack(
        [
            starts[0] + jnp.arange(half, dtype=jnp.int32),
            starts[1] + jnp.arange(half, dtype=jnp.int32),
        ]
    )
    scale_factor = 1.0 / math.sqrt(width)
    start_state = (
        jnp.full((2, groups, per_group, half), neg_large, jnp.float32),
        jnp.zeros((2, groups, per_group, half), jnp.float32),
        jnp.zeros((2, half, groups, per_group, width), jnp.float32),
    )
    carried_memory = start_state
    key_part = lax.all_gather(mentor_address_vectors, "seq", axis=0, tiled=True)
    value_part = lax.all_gather(mentor_content_vectors, "seq", axis=0, tiled=True)
    piece_len = key_part.shape[0]
    block_len = math.gcd(512, piece_len)
    blocks = piece_len // block_len
    key_blocks = key_part.reshape(blocks, block_len, groups, width)
    value_blocks = value_part.reshape(blocks, block_len, groups, width)
    block_starts = jnp.arange(blocks, dtype=jnp.int32) * block_len

    def visit(state_now, item):
        key_block, value_block, first_key = item
        key_pos = first_key + jnp.arange(block_len, dtype=jnp.int32)
        row_max, row_sum, accum = state_now
        maxes = []
        sums = []
        accums = []
        for member in range(2):

            def update(parts, member=member):
                old_max, old_sum, old_acc = parts
                scores = (
                    jnp.einsum(
                        "qghd,kgd->ghqk",
                        query_halves[member],
                        key_block,
                        preferred_element_type=jnp.float32,
                    )
                    * scale_factor
                )
                visible = query_pos[member][:, None] >= key_pos[None, :]
                scores = jnp.where(visible, scores, neg_large)
                new_max = jnp.maximum(old_max, jnp.max(scores, axis=-1))
                probs = jnp.where(visible, jnp.exp(scores - new_max[..., None]), 0.0)
                rescale = jnp.exp(old_max - new_max)
                new_sum = old_sum * rescale + jnp.sum(probs, axis=-1)
                new_acc = old_acc * jnp.transpose(rescale, (2, 0, 1))[..., None] + jnp.einsum(
                    "ghqk,kgd->qghd",
                    probs.astype(jnp.bfloat16),
                    value_block,
                    preferred_element_type=jnp.float32,
                )
                return (new_max, new_sum, new_acc)

            needed = first_key <= query_pos[member, half - 1]
            result = lax.cond(
                needed, update, keep_same, (row_max[member], row_sum[member], accum[member])
            )
            maxes.append(result[0])
            sums.append(result[1])
            accums.append(result[2])
        return ((jnp.stack(maxes), jnp.stack(sums), jnp.stack(accums)), None)

    carried_memory, unused = lax.scan(
        visit, carried_memory, (key_blocks, value_blocks, block_starts)
    )
    row_max, row_sum, accum = carried_memory
    normed = accum / jnp.transpose(row_sum, (0, 3, 1, 2))[..., None]
    return normed.astype(jnp.bfloat16).reshape(2, half, groups * per_group, width)


def shards(
    probe_vectors,
    mentor_address_vectors,
    mentor_content_vectors,
    previous_position_blend,
    feature_fading_exponent,
    fading_narrowing_matrix,
    fading_widening_matrix,
    diagonal_extra_amount,
):
    tok_rows = probe_vectors.shape[0]
    heads = previous_position_blend.shape[1]
    width = previous_position_blend.shape[2]
    groups = mentor_address_vectors.shape[1] // width
    per_group = heads // groups
    half = tok_rows // 2
    place = lax.axis_index("seq")
    count = lax.axis_size("seq")
    query_prev, key_prev, value_prev = passed_along(
        (probe_vectors[-1:], mentor_address_vectors[-1:], mentor_content_vectors[-1:]), "seq", 1
    )
    own_start = place * tok_rows
    starts = (own_start, own_start + half)
    teacher_halves = attend(
        probe_vectors,
        starts,
        mentor_address_vectors,
        mentor_content_vectors,
        groups,
        per_group,
        width,
    )
    teacher_out = teacher_halves.reshape(tok_rows, heads, width)

    def with_previous(current, prev_row):
        return jnp.concatenate([prev_row, current[:-1]], axis=0)

    def local_parts(rotary_angle):
        (
            lagged_blend_fractions,
            fading_exponent_start,
            narrowing_product,
            widening_product,
            diagonal_extra_vector,
        ) = rotary_angle
        query_f = probe_vectors.astype(jnp.float32).reshape(tok_rows, heads, width)
        query_p = with_previous(query_f, query_prev.astype(jnp.float32).reshape(1, heads, width))
        key_g = mentor_address_vectors.astype(jnp.float32).reshape(tok_rows, groups, width)
        key_p = with_previous(key_g, key_prev.astype(jnp.float32).reshape(1, groups, width))
        value_g = mentor_content_vectors.astype(jnp.float32).reshape(tok_rows, groups, width)
        value_p = with_previous(value_g, value_prev.astype(jnp.float32).reshape(1, groups, width))
        key_f = jnp.repeat(key_g, per_group, axis=1)
        key_pf = jnp.repeat(key_p, per_group, axis=1)
        value_f = jnp.repeat(value_g, per_group, axis=1)
        value_pf = jnp.repeat(value_p, per_group, axis=1)
        gate_vectors = query_f + lagged_blend_fractions[0] * (query_p - query_f)
        lagged_address_blend = key_f + lagged_blend_fractions[1] * (key_pf - key_f)
        lagged_content_blend = value_f + lagged_blend_fractions[2] * (value_pf - value_f)
        decay_input = query_f + lagged_blend_fractions[3] * (query_p - query_f)
        low_rank_decay = jnp.tanh(
            jnp.einsum("ydj,dja->yda", decay_input, narrowing_product, precision=highest_precision)
        )
        token_log_decay = -jnp.exp(
            fading_exponent_start
            + jnp.einsum(
                "dby,byp->dbp", low_rank_decay, widening_product, precision=highest_precision
            )
        )
        block_len = math.gcd(32, tok_rows)
        blocks = tok_rows // block_len

        def split_blocks(array_in):
            return array_in.reshape(blocks, block_len, heads, width)

        def advance(carried_memory, hidden_activations):
            return jax.checkpoint(segment_carry_forward)(
                diagonal_extra_vector, carried_memory, hidden_activations
            )

        start_state = (
            jnp.zeros((heads, width, width), jnp.float32),
            jnp.zeros((heads, width), jnp.float32),
        )
        final_state, outputs = lax.scan(
            advance,
            start_state,
            (
                split_blocks(gate_vectors),
                split_blocks(lagged_address_blend),
                split_blocks(lagged_content_blend),
                split_blocks(token_log_decay),
            ),
        )
        local_out = outputs[0].reshape(tok_rows, heads, width)
        rate_rows = outputs[1].reshape(tok_rows, heads, width)
        return (local_out, rate_rows, final_state[1], final_state[0])

    rotary_angle = (
        previous_position_blend,
        feature_fading_exponent,
        fading_narrowing_matrix,
        fading_widening_matrix,
        diagonal_extra_amount,
    )
    parts_out, pullback = jax.vjp(local_parts, rotary_angle)
    local_out, rate_rows, log_total, state_local = parts_out
    fade = jnp.exp(log_total)
    identity = (jnp.ones_like(fade), jnp.zeros_like(state_local))
    unused_fade, state_in = prefix((fade, state_local), "seq", link_states, identity, False)
    student_out = local_out + jnp.einsum(
        "thi,hij->thj", rate_rows, state_in, precision=highest_precision
    )
    student_norm, norm_pullback = jax.vjp(group_norm, student_out)
    grad_norm = 2.0 * (student_norm - teacher_out.astype(jnp.float32)) / (tok_rows * count)
    (grad_out,) = norm_pullback(grad_norm)
    own_cot = jnp.einsum("thi,thj->hij", rate_rows, grad_out, precision=highest_precision)
    unused_back, later_cot = prefix((fade, own_cot), "seq", link_states, identity, True)
    grad_rates = jnp.einsum("thj,hij->thi", grad_out, state_in, precision=highest_precision)
    grad_log = jnp.sum(later_cot * state_in, axis=-1) * fade
    (grads,) = pullback((grad_out, grad_rates, grad_log, later_cot))
    summed = lax.psum((grads[0], grads[1], grads[2], grads[3], grads[4]), "seq")
    return (summed[0], summed[1], summed[2], summed[3], summed[4])


def solution(mesh):
    return jax.shard_map(
        shards,
        mesh=mesh,
        in_specs=(
            P("seq", "head"),
            P("seq", "head"),
            P("seq", "head"),
            P(None, "head", None),
            P("head", None),
            P("head", None, None),
            P("head", None, None),
            P("head", None),
        ),
        out_specs=(
            P(None, "head", None),
            P("head", None),
            P("head", None, None),
            P("head", None, None),
            P("head", None),
        ),
        check_vma=False,
    )
```

profile of v0, /device:TPU:0, one launch (start us, length us, event | category | flops | bytes accessed | tf_op | source)
XLA Modules:
  0.0 900.8 jit_solution(6714319771397736963)
XLA Ops:
  9.4 5.4 collective-permute-start
  52.1 111.2 %while.100 = (s32[]{:T(128)}, f32[16,128,128]{2,1,0:T(8,128)S(1)}, f32[16,128]{1,0:T(8,128)S(1)}, f32[4,32,16,128]{3,1,0,2:T(8,128)}, f32[4,32,16,128]{3,2,1,0:T...) while((s32[]{:T(128)}, f32[16,128,128]{2,1,0:T(8,128)S(1)}, ...), condition=%wide.region_3.4_spmd.clone.clone, body=%wide.region_0.3_spmd.clone.clone.sunk | while | flops 243256832 | bytes 32433352 | solution.py:254
  55.4 4.3 select_bitcast_fusion.2
  62.7 9.9 %fusion.224 = f32[16,32,32]{1,2,0:T(8,128)S(1)} fusion(f32[16,32,32,128]{3,0,2,1:T(8,128)} %select_bitcast_fusion.2, f32[16,128,32]{1,2,0:T(8,128)S(1)} %copy.352, f32[16,128,32]{1,2,0:T(8,128)S(1)} %copy.353), kind=kLoop, calls=%fused_computation.153.clone.1 | loop fusion | flops 6275072 | bytes 8978432 | tf_op jit(solution)/shard_map/jvp()/while/body/eval_jaxpr/thi,shi,tshi->hts/dot_general | solution.py:65
  83.1 4.3 select_bitcast_fusion.2
  90.4 9.8 %fusion.224 = f32[16,32,32]{1,2,0:T(8,128)S(1)} fusion(f32[16,32,32,128]{3,0,2,1:T(8,128)} %select_bitcast_fusion.2, f32[16,128,32]{1,2,0:T(8,128)S(1)} %copy.352, f32[16,128,32]{1,2,0:T(8,128)S(1)} %copy.353), kind=kLoop, calls=%fused_computation.153.clone.1 | loop fusion | flops 6275072 | bytes 8978432 | tf_op jit(solution)/shard_map/jvp()/while/body/eval_jaxpr/thi,shi,tshi->hts/dot_general | solution.py:65
  110.8 4.3 select_bitcast_fusion.2
  118.1 10.1 %fusion.224 = f32[16,32,32]{1,2,0:T(8,128)S(1)} fusion(f32[16,32,32,128]{3,0,2,1:T(8,128)} %select_bitcast_fusion.2, f32[16,128,32]{1,2,0:T(8,128)S(1)} %copy.352, f32[16,128,32]{1,2,0:T(8,128)S(1)} %copy.353), kind=kLoop, calls=%fused_computation.153.clone.1 | loop fusion | flops 6275072 | bytes 8978432 | tf_op jit(solution)/shard_map/jvp()/while/body/eval_jaxpr/thi,shi,tshi->hts/dot_general | solution.py:65
  138.8 4.3 select_bitcast_fusion.2
  146.1 9.8 %fusion.224 = f32[16,32,32]{1,2,0:T(8,128)S(1)} fusion(f32[16,32,32,128]{3,0,2,1:T(8,128)} %select_bitcast_fusion.2, f32[16,128,32]{1,2,0:T(8,128)S(1)} %copy.352, f32[16,128,32]{1,2,0:T(8,128)S(1)} %copy.353), kind=kLoop, calls=%fused_computation.153.clone.1 | loop fusion | flops 6275072 | bytes 8978432 | tf_op jit(solution)/shard_map/jvp()/while/body/eval_jaxpr/thi,shi,tshi->hts/dot_general | solution.py:65
  169.7 38.3 %all-gather = f32[256,128]{1,0:T(8,128)S(1)} all-gather(f32[16,128]{1,0:T(8,128)S(1)} %exp.110), channel_id=2, replica_groups=mesh['seq'=16,'head'=2] {'seq'}, dimensions={0}, use_global_device_ids=true | all-gather | bytes 139264 | tf_op jit(solution)/shard_map/all_gather | solution.py:21
  217.1 58.4 %while.96 = (s32[]{:T(128)}, f32[2,4,4,64]{3,2,1,0:T(4,128)S(1)}, f32[2,4,4,64]{3,2,1,0:T(4,128)S(1)}, f32[2,64,4,4,128]{4,1,3,2,0:T(8,128)}, s32[4]{0:T(128)S(1...) while((s32[]{:T(128)}, f32[2,4,4,64]{3,2,1,0:T(4,128)S(1)}, ...), condition=%wide.region_17.18_spmd.clone, body=%wide.region_8.17_spmd.clone.sunk | while | flops 551365248 | bytes 34546184 | solution.py:163
  224.3 6.0 conditional.7
  232.9 6.0 conditional.6
  277.2 79.6 %all-gather.12.cloned.1.call-done = f32[256,128,128]{2,1,0:T(8,128)} async-done(((f32[16,128,128]{2,1,0:T(8,128)}), f32[256,128,128]{2,1,0:T(8,128)}) %all-gather.12.cloned.1.call-update) | async-done | bytes 16777232 | tf_op jit(solution)/shard_map/all_gather | solution.py:21
  356.8 30.3 %while.97 = (s32[]{:T(128)}, f32[16,128,128]{2,1,0:T(8,128)S(1)}, s32[]{:T(128)}, f32[16,16,128]{2,1,0:T(8,128)S(1)}, f32[16,16,128,128]{3,2,1,0:T(8,128)}, /*index=5*/s32[]{:T(128)}, s32[]{:T(128)}) while((s32[]{:T(128)}, f32[16,128,128]{2,1,0:T(8,128)S(1)}, s32[]{:T(128)}, f32[16,16,128]{2,1,0:T(8,128)S(1)}, ...), condition=%wide.region_5.6_spmd.clone, body=%wide.region_4.5_spmd.clone.sunk | while | flops 1048580 | bytes 3170409 | solution.py:32
  398.9 4.5 fusion.132
  403.5 185.3 %all-gather.14.cloned.1.call-done = f32[256,128,128]{2,1,0:T(8,128)} async-done(((f32[16,128,128]{2,1,0:T(8,128)}), f32[256,128,128]{2,1,0:T(8,128)}) %all-gather.14.cloned.1.call-update) | async-done | bytes 16777232 | tf_op jit(solution)/shard_map/all_gather | solution.py:21
  588.8 30.5 %while.98 = (s32[]{:T(128)}, f32[16,128,128]{2,1,0:T(8,128)S(1)}, s32[]{:T(128)}, f32[16,16,128]{2,1,0:T(8,128)S(1)}, f32[16,16,128,128]{3,2,1,0:T(8,128)}, /*index=5*/s32[]{:T(128)}, s32[]{:T(128)}, s32[]{:T(128)}, s32[]{:T(128)}) while((s32[]{:T(128)}, f32[16,128,128]{2,1,0:T(8,128)S(1)}, s32[]{:T(128)}, ...), condition=%wide.region_21.22_spmd.clone, body=%wide.region_20.21_spmd.clone.sunk | while | flops 1048584 | bytes 3170471 | solution.py:32
  623.2 148.7 %while.99 = (s32[]{:T(128)}, f32[16,128]{1,0:T(8,128)S(1)}, f32[16,128,128]{2,1,0:T(8,128)S(1)}, f32[16,128]{1,0:T(8,128)S(1)}, f32[4,32,16,128]{3,2,1,0:T(8,128...) while((s32[]{:T(128)}, f32[16,128]{1,0:T(8,128)S(1)}, ...), condition=%wide.region_34.35_spmd.clone, body=%wide.region_23.34_spmd.clone.sunk | while | flops 517592192 | bytes 33404152 | solution.py:254
  631.8 4.7 fusion.211
  636.5 5.8 fusion.210
  642.3 4.1 fusion.208
  668.9 4.7 fusion.211
  673.6 5.8 fusion.210
  679.4 4.1 fusion.208
  706.0 4.7 fusion.211
  710.7 5.8 fusion.210
  743.1 4.7 fusion.211
  747.8 5.8 fusion.210
  786.0 74.8 %all-reduce.5 = (f32[4,16,128]{2,1,0:T(8,128)}, f32[16,128]{1,0:T(8,128)}, f32[16,128]{1,0:T(8,128)}) all-reduce(f32[4,16,128]{2,1,0:T(8,128)S(1)} %pad_add_fusion, f32[16,128]{1,0:T(8,128)S(1)} %get-tuple-element.1468, f32[16,128]{1,0:T(8,128)S(1)} %get-tuple-element.914), channel_id=1, replica_groups=mesh['seq'=16,'head'=2] {'seq'}, use_global_device_ids=true, to_apply=%region_39.40 | all-reduce | flops 12288 | bytes 98304 | tf_op jit(solution)/shard_map/psum | solution.py:291
  860.9 29.4 %all-reduce.9.cloned.1.call-done = (f32[16,128,64]{1,2,0:T(8,128)}, f32[16,64,128]{2,1,0:T(8,128)}) async-done(((f32[16,128,64]{1,2,0:T(8,128)}, f32[16,64,128]{2,1,0:T(8,128)}), (f32[16,128,64]{1,2,0:T(8,128)}, f32[16,64,128]{2,1,0:T(8,128)})) %all-reduce.9.cloned.1.call-update) | async-done | bytes 1048592 | tf_op jit(solution)/shard_map/psum | solution.py:291
  (512 shorter events, 348.4 us)
Async XLA Ops:
  7.2 36.9 %copy-start = (f32[16,64,128]{2,1,0:T(8,128)S(1)}, f32[16,64,128]{2,1,0:T(8,128)}, u32[]{:S(2)}) copy-start(f32[16,64,128]{2,1,0:T(8,128)} %param.28) | copy-start | bytes 1572868
  7.2 23.0 %copy-start.26 = (bf16[128,512]{1,0:T(8,128)(2,1)S(1)}, bf16[128,512]{1,0:T(8,128)(2,1)}, u32[]{:S(2)}) copy-start(bf16[128,512]{1,0:T(8,128)(2,1)} %param.23) | copy-start | bytes 393220
  7.2 23.1 %copy-start.27 = (bf16[128,512]{1,0:T(8,128)(2,1)S(1)}, bf16[128,512]{1,0:T(8,128)(2,1)}, u32[]{:S(2)}) copy-start(bf16[128,512]{1,0:T(8,128)(2,1)} %param.24) | copy-start | bytes 393220
  7.2 200.8 %all-gather.8.cloned.1.call-start = ((), (), s32[]{:S(2)}) async-start(), calls=%async_computation | async-start | bytes 2228224 | tf_op jit(solution)/shard_map/all_gather | solution.py:111
  7.9 204.1 %all-gather.10.cloned.1.call-start = ((), (), s32[]{:S(2)}) async-start(), calls=%async_computation.1 | async-start | bytes 2228224 | tf_op jit(solution)/shard_map/all_gather | solution.py:112
  9.4 30.8 %collective-permute-start = (bf16[1,2048]{1,0:T(2,128)(2,1)}, bf16[1,2048]{1,0:T(2,128)(2,1)}, u32[]{:S(2)}, u32[]{:S(2)}) collective-permute-start(bf16[1,2048]{1,0:T(2,128)(2,1)} %slice.85), channel_id=1, source_target_pairs={{0,2},{2,4},{4,6},{6,8},{8,10},{10,12},{12,14},{14,16},{16,18},{18... | collective-permute-start | bytes 12296 | tf_op jit(solution)/shard_map/ppermute | solution.py:16
  16.1 23.9 %collective-permute-start.1 = (bf16[1,512]{1,0:T(2,128)(2,1)}, bf16[1,512]{1,0:T(2,128)(2,1)S(1)}, u32[]{:S(2)}, u32[]{:S(2)}) collective-permute-start(bf16[1,512]{1,0:T(2,128)(2,1)} %slice.89), channel_id=1, source_target_pairs={{0,2},{2,4},{4,6},{6,8},{8,10},{10,12},{12,14},{14,16},{16,18},{18... | collective-permute-start | bytes 3080 | tf_op jit(solution)/shard_map/ppermute | solution.py:16
  20.2 17.5 %collective-permute-start.2 = (bf16[1,512]{1,0:T(2,128)(2,1)}, bf16[1,512]{1,0:T(2,128)(2,1)}, u32[]{:S(2)}, u32[]{:S(2)}) collective-permute-start(bf16[1,512]{1,0:T(2,128)(2,1)} %slice.93), channel_id=1, source_target_pairs={{0,2},{2,4},{4,6},{6,8},{8,10},{10,12},{12,14},{14,16},{16,18},{18... | collective-permute-start | bytes 3080 | tf_op jit(solution)/shard_map/ppermute | solution.py:16
  24.2 332.6 %all-gather.12.cloned.1.call-start = ((), (), s32[]{:S(2)}) async-start(), calls=%async_computation.2 | async-start | bytes 17825792 | tf_op jit(solution)/shard_map/all_gather | solution.py:21
  27.9 13.1 %copy-start.30 = (f32[16,128]{1,0:T(8,128)}, f32[16,128]{1,0:T(8,128)S(1)}, u32[]{:S(2)}) copy-start(f32[16,128]{1,0:T(8,128)S(1)} %get-tuple-element.1506) | copy-start | bytes 24580
  32.3 5.2 copy-start.29
  32.3 6.3 copy-start.34
  41.0 6.6 copy-start.8
  41.1 6.6 copy-start.14
  41.1 6.5 copy-start.12
  41.1 6.5 copy-start.32
  41.1 6.5 copy-start.33
  62.7 9.9 %copy-start.4 = (f32[32,16,128]{2,1,0:T(8,128)S(1)}, f32[32,16,128]{2,1,0:T(8,128)}, u32[]{:S(2)}) copy-start(f32[32,16,128]{2,1,0:T(8,128)} %get-tuple-element.1932) | copy-start | bytes 786436 | tf_op jit(solution)/shard_map/jvp()/while
  90.4 9.9 %copy-start.4 = (f32[32,16,128]{2,1,0:T(8,128)S(1)}, f32[32,16,128]{2,1,0:T(8,128)}, u32[]{:S(2)}) copy-start(f32[32,16,128]{2,1,0:T(8,128)} %get-tuple-element.1932) | copy-start | bytes 786436 | tf_op jit(solution)/shard_map/jvp()/while
  118.1 10.1 %copy-start.4 = (f32[32,16,128]{2,1,0:T(8,128)S(1)}, f32[32,16,128]{2,1,0:T(8,128)}, u32[]{:S(2)}) copy-start(f32[32,16,128]{2,1,0:T(8,128)} %get-tuple-element.1932) | copy-start | bytes 786436 | tf_op jit(solution)/shard_map/jvp()/while
  146.1 9.9 %copy-start.4 = (f32[32,16,128]{2,1,0:T(8,128)S(1)}, f32[32,16,128]{2,1,0:T(8,128)}, u32[]{:S(2)}) copy-start(f32[32,16,128]{2,1,0:T(8,128)} %get-tuple-element.1932) | copy-start | bytes 786436 | tf_op jit(solution)/shard_map/jvp()/while
  163.3 48.7 %copy-start.3 = (f32[4,32,16,128]{3,1,2,0:T(8,128)}, f32[4,32,16,128]{3,1,2,0:T(8,128)S(1)}, u32[]{:S(2)}) copy-start(f32[4,32,16,128]{3,1,2,0:T(8,128)S(1)} %get-tuple-element.2181) | copy-start | bytes 3145732
  164.3 424.5 %all-gather.14.cloned.1.call-start = ((), (), s32[]{:S(2)}) async-start(), calls=%async_computation.3 | async-start | bytes 17825792 | tf_op jit(solution)/shard_map/all_gather | solution.py:21
  217.1 5.2 copy-start.2
  240.7 5.1 copy-start.2
  252.3 5.1 copy-start.2
  263.9 5.1 copy-start.2
  390.7 6.0 copy-start.16
  398.8 491.4 %all-reduce.9.cloned.1.call-start = ((), (), s32[]{:S(2)}) async-start(), calls=%async_computation.4 | async-start | bytes 2097152 | tf_op jit(solution)/shard_map/psum | solution.py:291
  780.0 5.3 copy-start.13
  780.0 5.3 copy-start.15
  780.0 5.3 copy-start.22
  (18 other events, 54.2 us)
Sparse Core Ops, SparseCore 0:
  10.8 63.4 all-gather.7
  77.0 59.3 all-gather.9
  164.5 192.3 all-gather.11
  399.0 189.7 all-gather.13
  780.1 110.1 all-reduce.8
where the time goes:
time: 912 us; the launch traced here: 901 us
  waiting for transfers between devices  295 us (32%)
  other arithmetic  252 us (28%)
  blocking collectives  113 us (12%)
  local copies, waits for them, and re-layouts  112 us (12%)
  matrix products  87.5 us (10%)
  between operations  14.8 us (2%)
  loops' own time  13.3 us (1%)
  starting transfers between devices  12.8 us (1%)
    all_gather x2, waiting for transfers between devices, prefix(): everything = jax.tree.map(lambda part: lax.all_gather(part, axis), x)  265 us
    dot_general x16, other arithmetic, segment_carry_forward(): jnp.einsum('thi,shi,tshi->hts', gate_vectors, lagged_address_blend, facto...  87.3 us
    psum x1, blocking collectives, shards(): summed = lax.psum((grads[0], grads[1], grads[2], grads[3], grads[4]), 'seq')  74.8 us
    select_n x32, other arithmetic, lap(): return jax.tree.map(lambda a, b: jnp.where(reached, a, b), new, before)  59.3 us
    all_gather x1, blocking collectives, prefix(): everything = jax.tree.map(lambda part: lax.all_gather(part, axis), x)  38.3 us
    psum x1, waiting for transfers between devices, shards(): summed = lax.psum((grads[0], grads[1], grads[2], grads[3], grads[4]), 'seq')  29.4 us
    squeeze x36, local copies, waits for them, and re-layouts, local_parts(): lax.scan(advance, start_state, (split_blocks(gate_vectors), split_blocks(...  25.5 us
    reduce_sum x4, other arithmetic, segment_carry_forward(): spread = jnp.where(before, exclusive[:, None] - inclusive[None, :], 0.0)  23.1 us
  transfers between devices with their start and end apart: 8, of which 3 were waited for; matrix products, arithmetic and copies ran while one was open for 24% of the time, Pallas kernels for 0%

commit v1 on v0

v1 whole, which is shorter than its diff:
```python
import math

import jax
import jax.numpy as jnp
from jax import lax
from jax.experimental import pallas as pl
from jax.experimental.pallas import tpu as pltpu
from jax.sharding import PartitionSpec as P

NORM_EPS = 0.00064
NEG_LARGE = -1e30
CHUNK = 128
SAFE_EXPONENT = 30.0
PACK_TAIL = 8

f32 = jnp.float32
bf16 = jnp.bfloat16

NN = (((1,), (0,)), ((), ()))
NT = (((1,), (1,)), ((), ()))
TN = (((0,), (0,)), ((), ()))


def dot(a, b, dims):
    return lax.dot_general(a, b, dims, preferred_element_type=f32)


def split2(x):
    high = x.astype(bf16)
    return high, (x - high.astype(f32)).astype(bf16)


def split3(x):
    high = x.astype(bf16)
    rest = x - high.astype(f32)
    middle = rest.astype(bf16)
    return high, middle, (rest - middle.astype(f32)).astype(bf16)


def dot3(a, b, dims):
    return dot(a[0], b[0], dims) + (dot(a[0], b[1], dims) + dot(a[1], b[0], dims))


def dot4(a, b, dims):
    return dot(a[0], b[0], dims) + (
        (dot(a[0], b[1], dims) + dot(a[1], b[0], dims)) + dot(a[1], b[1], dims)
    )


def joined(parts):
    return parts[0].astype(f32) + parts[1].astype(f32)


def exact_sums(zero_one, x):
    high, middle, low = split3(x)
    return dot(zero_one, high, NN) + (dot(zero_one, middle, NN) + dot(zero_one, low, NN))


def row_ids(shape):
    return lax.broadcasted_iota(jnp.int32, shape, 0)


def lane_ids(shape):
    return lax.broadcasted_iota(jnp.int32, shape, 1)


def zero_one(condition):
    return jnp.where(condition, 1.0, 0.0).astype(bf16)


def with_shift(ref, start, rows):
    now = ref[pl.ds(start, rows), :].astype(f32)
    tail = ref[pl.ds(pl.multiple_of(jnp.maximum(start - 16, 0), 16), 16), :].astype(f32)[15:16]
    tail = jnp.where(start > 0, tail, 0.0)
    earlier = jnp.where(row_ids(now.shape) == 0, tail, pltpu.roll(now, 1, 0))
    return now, earlier - now


def teacher_phase(q_ref, k_ref, v_ref, teach, scores, q_rows, k_rows):
    tokens, width = q_ref.shape
    scale = 1.0 / math.sqrt(width)

    def q_block(i, _):
        start = pl.multiple_of(i * q_rows, q_rows)
        q = q_ref[pl.ds(start, q_rows), :]
        blocks = (start + q_rows + k_rows - 1) // k_rows

        def score_block(j, top):
            first = pl.multiple_of(j * k_rows, k_rows)
            s = dot(q, k_ref[pl.ds(first, k_rows), :], NT) * scale
            seen = start + row_ids(s.shape) >= first + lane_ids(s.shape)
            s = jnp.where(seen, s, NEG_LARGE)
            scores[j] = s
            for n in range(k_rows // 128):
                top = jnp.maximum(top, s[:, n * 128 : (n + 1) * 128])
            return top

        top = lax.fori_loop(0, blocks, score_block, jnp.full((q_rows, 128), NEG_LARGE, f32))
        row_top = jnp.max(top, axis=1, keepdims=True)

        def value_block(j, carry):
            total, accum = carry
            first = pl.multiple_of(j * k_rows, k_rows)
            p = jnp.exp(scores[j] - row_top)
            for n in range(k_rows // 128):
                total = total + p[:, n * 128 : (n + 1) * 128]
            return total, accum + dot(p.astype(bf16), v_ref[pl.ds(first, k_rows), :], NN)

        total, accum = lax.fori_loop(
            0,
            blocks,
            value_block,
            (jnp.zeros((q_rows, 128), f32), jnp.zeros((q_rows, width), f32)),
        )
        teach[pl.ds(start, q_rows), :] = (accum / jnp.sum(total, axis=1, keepdims=True)).astype(
            bf16
        )
        return 0

    lax.fori_loop(0, tokens // q_rows, q_block, 0)


def decay_phase(q_ref, down, up, fade, mix, lw_s, ex_s, hid_s, rows):
    tokens, width = q_ref.shape
    square = (CHUNK, CHUNK)
    before = zero_one(row_ids(square) > lane_ids(square))

    def block(i, worst):
        start = pl.multiple_of(i * rows, rows)
        q, q_step = with_shift(q_ref, start, rows)
        hid = jnp.tanh(dot3(split2(q + mix[3] * q_step), down, NN))
        lw = -jnp.exp(fade + dot3(split2(hid), up, NN))
        hid_s[pl.ds(start, rows), :] = hid
        lw_s[pl.ds(start, rows), :] = lw
        for n in range(rows // CHUNK):
            part = lw[n * CHUNK : (n + 1) * CHUNK]
            ex = exact_sums(before, part)
            ex_s[pl.ds(pl.multiple_of(start + n * CHUNK, CHUNK), CHUNK), :] = ex
            middle = ex[CHUNK // 2 : CHUNK // 2 + 1]
            total = ex[CHUNK - 1 :] + part[CHUNK - 1 :]
            worst = jnp.maximum(worst, jnp.maximum(-middle, middle - total))
        return worst

    return lax.fori_loop(0, tokens // rows, block, jnp.zeros((1, width), f32))


def level_parts(level, lw, r, k):
    square = (CHUNK, CHUNK)
    t, m = row_ids(square), lane_ids(square)
    edge = ((t >> (level + 1)) << (level + 1)) + (1 << level) - 1
    upper = ((t >> level) & 1) == 1
    lower = ((t >> level) & 1) == 0
    span = zero_one((upper & (m > edge) & (m < t)) | (lower & (m > t) & (m <= edge)))
    factor = jnp.exp(exact_sums(span, lw))
    upper_rows = ((row_ids(r.shape) >> level) & 1) == 1
    r_factor = jnp.where(upper_rows, factor, 0.0)
    k_factor = jnp.where(upper_rows, 0.0, factor)
    same = (t >> (level + 1)) == (m >> (level + 1))
    return r_factor, k_factor, split2(r * r_factor), split2(k * k_factor), same, span


def student_phase(fast, refs, mix, bonus, down, up, scratch, out_ref, unroll):
    q_ref, k_ref, v_ref = refs
    teach, lw_s, ex_s, hid_s, state_s, g_s, a_hi_s, a_lo_s = scratch
    tokens, width = q_ref.shape
    chunks = tokens // CHUNK
    levels = CHUNK.bit_length() - 1
    square = (CHUNK, CHUNK)
    t, m = row_ids(square), lane_ids(square)
    below = t > m
    after, before = zero_one(t < m), zero_one(below)
    gain = 2.0 / tokens

    def load(c):
        start = pl.multiple_of(c * CHUNK, CHUNK)
        rows = pl.ds(start, CHUNK)
        q, q_step = with_shift(q_ref, start, CHUNK)
        k0, k_step = with_shift(k_ref, start, CHUNK)
        v0, v_step = with_shift(v_ref, start, CHUNK)
        r = q + mix[0] * q_step
        k = k0 + mix[1] * k_step
        v = v0 + mix[2] * v_step
        lw, ex = lw_s[rows, :], ex_s[rows, :]
        total = ex[CHUNK - 1 :] + lw[CHUNK - 1 :]
        if fast:
            middle = ex[CHUNK // 2 : CHUNK // 2 + 1]
            r_factor = jnp.exp(ex - middle)
            k_factor = jnp.exp(middle - ex - lw)
            into, out = jnp.exp(middle), jnp.exp(total - middle)
        else:
            r_factor = jnp.exp(ex)
            k_factor = jnp.exp(exact_sums(after, lw))
            into = out = None
        return rows, q, q_step, k_step, v_step, r, k, v, lw, total, r_factor, k_factor, into, out

    def scaled(x, by):
        return x if by is None else x * by

    def forward(c, state):
        rows, _, _, _, _, r, k, v, lw, total, r_factor, k_factor, into, out = load(c)
        rs, ks, vs = split2(r * r_factor), split2(k * k_factor), split2(v)
        if fast:
            a = jnp.where(below, dot3(rs, ks, NT), 0.0)
        else:

            def one_level(level, a):
                _, _, r_part, k_part, block, _ = level_parts(level, lw, r, k)
                return a + jnp.where(block, dot3(r_part, k_part, NT), 0.0)

            a = lax.fori_loop(0, levels, one_level, jnp.zeros(square, f32))
        own = jnp.sum(r * bonus * k, axis=1, keepdims=True)
        a = split2(a)
        state_s[c] = state
        o = own * v + dot3(a, vs, NN) + dot3(rs, split2(scaled(state, into)), NT)
        o = o - jnp.mean(o, axis=1, keepdims=True)
        rate = lax.rsqrt(jnp.mean(o * o, axis=1, keepdims=True) + NORM_EPS)
        normed = o * rate
        g = gain * (normed - teach[rows, :].astype(f32))
        g = g - jnp.mean(g, axis=1, keepdims=True) - normed * jnp.mean(
            g * normed, axis=1, keepdims=True
        )
        g_s[rows, :] = g * rate
        a_hi_s[rows, :] = a[0]
        a_lo_s[rows, :] = a[1]
        return state * jnp.exp(total) + scaled(dot3(vs, ks, TN), out)

    def forward_some(i, state):
        for n in range(unroll):
            state = forward(i * unroll + n, state)
        return state

    state = lax.fori_loop(0, chunks // unroll, forward_some, jnp.zeros((width, width), f32))
    state_s[chunks] = state

    def backward(c, carry):
        cot, up_sum, down_sum, sums = carry
        rows, q, q_step, k_step, v_step, r, k, v, lw, total, r_factor, k_factor, into, out = load(c)
        rs, ks, vs = split2(r * r_factor), split2(k * k_factor), split2(v)
        g = g_s[rows, :]
        gs = split2(g)
        a = (a_hi_s[rows, :], a_lo_s[rows, :])
        pair = dot3(gs, vs, NT)
        cot_out = split2(scaled(cot, out))
        dr = r_factor * dot3(gs, split2(scaled(state_s[c], into)), NN)
        dk = k_factor * dot3(vs, cot_out, NN)
        dv = dot3(a, gs, TN) + dot3(ks, cot_out, NT)
        from_later, from_earlier = r * dr, k * dk
        dlw = jnp.sum(state_s[c] * jnp.exp(total) * cot, axis=0, keepdims=True)
        if fast:
            pairs = split2(jnp.where(below, pair, 0.0))
            dr_in, dk_in = dot4(pairs, ks, NN), dot4(pairs, rs, TN)
            k_in = joined(ks) * dk_in
            from_later = from_later + (joined(rs) * dr_in - k_in)
            dlw = dlw - k_in
            dr = dr + r_factor * dr_in
            dk = dk + k_factor * dk_in
        else:

            def one_level(level, parts):
                dr, dk, dlw = parts
                r_by, k_by, r_part, k_part, block, span = level_parts(level, lw, r, k)
                pairs = split2(jnp.where(block & below, pair, 0.0))
                dr_in = r_by * dot3(pairs, k_part, NN)
                dk_in = k_by * dot3(pairs, r_part, TN)
                inside = split3(r * dr_in + k * dk_in)
                return dr + dr_in, dk + dk_in, dlw + sum(dot(span, part, TN) for part in inside)

            dr, dk, dlw = lax.fori_loop(
                0, levels, one_level, (dr, dk, jnp.broadcast_to(dlw, r.shape))
            )
        dlw = dlw + exact_sums(after, from_later) + exact_sums(before, from_earlier)
        dv = dv + jnp.sum(r * bonus * k, axis=1, keepdims=True) * g
        own = jnp.sum(v * g, axis=1, keepdims=True)
        own_r, own_k = own * r, own * k
        dr = dr + bonus * own_k
        dk = dk + bonus * own_r
        dpre = dlw * lw
        hid = hid_s[rows, :]
        dpres = split2(dpre)
        dz = dot3(dpres, up, NT) * (1.0 - hid * hid)
        dzs = split2(dz)
        dxw = dot3(dzs, down, NT)
        up_sum = up_sum + dot3(split2(hid), dpres, TN)
        down_sum = down_sum + dot3(dzs, split2(q + mix[3] * q_step), TN)
        parts = (dr * q_step, dk * k_step, dv * v_step, dxw * q_step, dpre, own_r * k)
        sums = tuple(
            old + jnp.sum(new.reshape(CHUNK // 8, 8, width), axis=0)
            for old, new in zip(sums, parts)
        )
        cot = cot * jnp.exp(total) + scaled(dot3(gs, rs, TN), into)
        return cot, up_sum, down_sum, sums

    def backward_some(i, carry):
        for n in range(unroll):
            carry = backward(chunks - 1 - (i * unroll + n), carry)
        return carry

    rank = hid_s.shape[1]
    empty = jnp.zeros((rank, width), f32)
    start = (jnp.zeros((width, width), f32), empty, empty, (jnp.zeros((8, width), f32),) * 6)
    _, up_sum, down_sum, sums = lax.fori_loop(0, chunks // unroll, backward_some, start)
    out_ref[:rank, :] = up_sum
    out_ref[rank : 2 * rank, :] = down_sum
    for n, part in enumerate(sums):
        out_ref[2 * rank + n : 2 * rank + n + 1, :] = jnp.sum(part, axis=0, keepdims=True)
    out_ref[2 * rank + 6 :, :] = jnp.zeros((PACK_TAIL - 6, width), f32)


def head_kernel(
    head_ref, qkv_ref, mix_ref, fade_ref, down_ref, up_ref, bonus_ref, out_ref, *scratch
):
    scores, teach, lw_s, ex_s, hid_s, *rest = scratch
    tokens = qkv_ref.shape[0]
    width = up_ref.shape[2]
    refs = tuple(qkv_ref.at[:, pl.ds(n * width, width)] for n in range(3))
    head = head_ref[0] + pl.program_id(0)
    mix = [mix_ref[n, pl.ds(head, 1), :] for n in range(4)]
    bonus = bonus_ref[pl.ds(head, 1), :]
    down, up = split2(down_ref[0]), split2(up_ref[0])
    rows = math.gcd(512, tokens)
    worst = decay_phase(
        refs[0], down, up, fade_ref[pl.ds(head, 1), :], mix, lw_s, ex_s, hid_s, rows
    )
    teacher_phase(*refs, teach, scores, math.gcd(256, tokens), math.gcd(512, tokens))
    safe = jnp.max(worst) <= SAFE_EXPONENT
    held = (teach, lw_s, ex_s, hid_s, *rest)

    @pl.when(safe)
    def _():
        student_phase(True, refs, mix, bonus, down, up, held, out_ref.at[0], 2)

    @pl.when(jnp.logical_not(safe))
    def _():
        student_phase(False, refs, mix, bonus, down, up, held, out_ref.at[0], 1)


def head_grads(qkv, first_head, mix, fade, down, up, bonus):
    tokens, columns = qkv.shape
    heads, width, rank = down.shape
    count = columns // (3 * width)
    whole = lambda *_: (0, 0)
    spec = pltpu.PrefetchScalarGridSpec(
        num_scalar_prefetch=1,
        grid=(count,),
        in_specs=[
            pl.BlockSpec((tokens, 3 * width), lambda i, h: (0, i)),
            pl.BlockSpec(mix.shape, lambda i, h: (0, 0, 0)),
            pl.BlockSpec(fade.shape, whole),
            pl.BlockSpec((1, width, rank), lambda i, h: (h[0] + i, 0, 0)),
            pl.BlockSpec((1, rank, width), lambda i, h: (h[0] + i, 0, 0)),
            pl.BlockSpec(bonus.shape, whole),
        ],
        out_specs=pl.BlockSpec((1, 2 * rank + PACK_TAIL, width), lambda i, h: (i, 0, 0)),
        scratch_shapes=[
            pltpu.VMEM(
                (tokens // math.gcd(512, tokens), math.gcd(256, tokens), math.gcd(512, tokens)), f32
            ),
            pltpu.VMEM((tokens, width), bf16),
            pltpu.VMEM((tokens, width), f32),
            pltpu.VMEM((tokens, width), f32),
            pltpu.VMEM((tokens, rank), f32),
            pltpu.VMEM((tokens // CHUNK + 1, width, width), f32),
            pltpu.VMEM((tokens, width), f32),
            pltpu.VMEM((tokens, CHUNK), bf16),
            pltpu.VMEM((tokens, CHUNK), bf16),
        ],
    )
    return pl.pallas_call(
        head_kernel,
        out_shape=jax.ShapeDtypeStruct((count, 2 * rank + PACK_TAIL, width), f32),
        grid_spec=spec,
        compiler_params=pltpu.CompilerParams(
            vmem_limit_bytes=58 * 1024 * 1024, dimension_semantics=("arbitrary",)
        ),
    )(first_head, qkv, mix, fade, down, up, bonus)


def shards(
    probe_vectors,
    mentor_address_vectors,
    mentor_content_vectors,
    previous_position_blend,
    feature_fading_exponent,
    fading_narrowing_matrix,
    fading_widening_matrix,
    diagonal_extra_amount,
):
    tok_rows = probe_vectors.shape[0]
    heads, width, rank = fading_narrowing_matrix.shape
    groups = mentor_address_vectors.shape[1] // width
    place = lax.axis_index("seq")
    count = lax.axis_size("seq")
    copies = max(1, count // heads)
    per_device = max(1, heads // count)
    assert heads * copies == per_device * count
    q = probe_vectors.reshape(tok_rows, heads, 1, width)
    k = jnp.repeat(
        mentor_address_vectors.reshape(tok_rows, groups, 1, width), heads // groups, axis=1
    )
    v = jnp.repeat(
        mentor_content_vectors.reshape(tok_rows, groups, 1, width), heads // groups, axis=1
    )
    qkv = jnp.concatenate([q, k, v], axis=2).reshape(tok_rows, heads, 3 * width)
    qkv = jnp.repeat(qkv, copies, axis=1).reshape(tok_rows, heads * copies * 3 * width)
    qkv = lax.all_to_all(qkv, "seq", split_axis=1, concat_axis=0, tiled=True)
    first_head = (place // copies) * per_device
    packed = head_grads(
        qkv,
        first_head.astype(jnp.int32).reshape(1),
        previous_position_blend,
        feature_fading_exponent,
        fading_narrowing_matrix,
        fading_widening_matrix,
        diagonal_extra_amount,
    )
    packed = lax.all_gather(packed, "seq", axis=0, tiled=True)[::copies]
    grad_up = packed[:, :rank]
    grad_down = jnp.swapaxes(packed[:, rank : 2 * rank], 1, 2)
    tail = packed[:, 2 * rank :]
    grad_mix = jnp.swapaxes(tail[:, :4], 0, 1)
    return grad_mix, tail[:, 4], grad_down, grad_up, tail[:, 5]


def solution(mesh):
    return jax.shard_map(
        shards,
        mesh=mesh,
        in_specs=(
            P("seq", "head"),
            P("seq", "head"),
            P("seq", "head"),
            P(None, "head", None),
            P("head", None),
            P("head", None, None),
            P("head", None, None),
            P("head", None),
        ),
        out_specs=(
            P(None, "head", None),
            P("head", None),
            P("head", None, None),
            P("head", None, None),
            P("head", None),
        ),
        check_vma=False,
    )
```

time: 912 us -> 170 us (0.19); the launches traced: 901 us -> 169 us
  other arithmetic: 252 us -> 1.31 us
  waiting for transfers between devices: 295 us -> 90.8 us
  blocking collectives: 113 us -> 0 us
  local copies, waits for them, and re-layouts: 112 us -> 11.7 us
  matrix products: 87.5 us -> 0 us
  Pallas kernels: 0 us -> 42.9 us
  loops' own time: 13.3 us -> 0 us
    all_gather x4 -> x1, waiting for transfers between devices: 265 us -> 58 us  [shards(): packed = lax.all_gather(packed, 'seq', axis=0, tiled=True)[::copies]]
    dot_general x49 -> x0, matrix products: 87.5 us -> none  [the longest x12 22.9 us: segment_carry_forward(): jnp.einsum('thi,hij->thj', gate_vectors * jnp.exp(exclusive), memory_matr...]
    dot_general x16 -> x0, other arithmetic: 87.3 us -> none  [segment_carry_forward(): jnp.einsum('thi,shi,tshi->hts', gate_vectors, lagged_address_blend, facto...]
    psum x1 -> x0, blocking collectives: 74.8 us -> none  [shards(): summed = lax.psum((grads[0], grads[1], grads[2], grads[3], grads[4]), 'seq')]
    select_n x32 -> x0, other arithmetic: 59.3 us -> none  [lap(): return jax.tree.map(lambda a, b: jnp.where(reached, a, b), new, before)]
    pallas_call x0 -> x1, Pallas kernels: none -> 42.9 us  [head_grads(): pl.pallas_call(head_kernel, out_shape=jax.ShapeDtypeStruct((count, 2 * ra...]
    all_gather x1 -> x0, blocking collectives: 38.3 us -> none  [prefix(): everything = jax.tree.map(lambda part: lax.all_gather(part, axis), x)]
    reduce_sum x26 -> x0, other arithmetic: 35.4 us -> none  [the longest x4 23.1 us: segment_carry_forward(): spread = jnp.where(before, exclusive[:, None] - inclusive[None, :], 0.0)]
  transfers between devices with their start and end apart: 8 -> 2, of which waited for: 3 -> 2; matrix products, arithmetic and copies ran while one was open for 24% -> 1% of each run, Pallas kernels for 0% -> 0%
where the time goes in v1:
time: 170 us; the launch traced here: 169 us
  waiting for transfers between devices  90.8 us (53%)
  Pallas kernels  42.9 us (25%)
  between operations  14.1 us (8%)
  local copies, waits for them, and re-layouts  11.7 us (7%)
  starting transfers between devices  8.49 us (5%)
    all_gather x1, waiting for transfers between devices, shards(): packed = lax.all_gather(packed, 'seq', axis=0, tiled=True)[::copies]  58 us
    pallas_call x1, Pallas kernels, head_grads(): pl.pallas_call(head_kernel, out_shape=jax.ShapeDtypeStruct((count, 2 * ra...  42.9 us
    all_to_all x1, waiting for transfers between devices, shards(): qkv = lax.all_to_all(qkv, 'seq', split_axis=1, concat_axis=0, tiled=True)  32.8 us
    all_to_all x1, starting transfers between devices, shards(): qkv = lax.all_to_all(qkv, 'seq', split_axis=1, concat_axis=0, tiled=True)  8.44 us
  transfers between devices with their start and end apart: 2, of which 2 were waited for; matrix products, arithmetic and copies ran while one was open for 1% of the time, Pallas kernels for 0%

profile of v1, /device:TPU:0, one launch (start us, length us, event | category | flops | bytes accessed | tf_op | source)
XLA Modules:
  0.0 169.3 jit_solution(16634987918770250308)
XLA Ops:
  7.2 1.0 copy.28
  8.2 1.0 copy.29
  9.2 1.3 copy.22
  10.5 0.1 broadcast_in_dim.10
  10.7 0.1 broadcast_in_dim.12
  10.8 1.3 pad_maximum_fusion
  12.1 0.0 copy-start
  12.1 8.4 %all-to-all-start = ((bf16[128,16,384]{0,2,1:T(8,128)(2,1)}), bf16[128,16,384]{0,2,1:T(8,128)(2,1)S(1)}, u32[]{:S(2)}, u32[]{:S(2)}) async-start(bf16[128,16,384]{0,2,1:T(8,128)(2,1)} %bitcast.6), calls=%async_computation | async-start | bytes 3145728 | tf_op jit(solution)/shard_map/all_to_all | solution.py:405
  20.5 0.0 all-gather.2.cloned.1.call-start
  20.6 0.0 copy-done
  20.6 1.3 copy.26.down_ref
  21.9 32.8 %all-to-all-done = bf16[128,16,384]{0,2,1:T(8,128)(2,1)S(1)} async-done(((bf16[128,16,384]{0,2,1:T(8,128)(2,1)}), bf16[128,16,384]{0,2,1:T(8,128)(2,1)S(1)}, u32[]{:S(2)}, u32[]{:S(2)}) %all-to-all-start) | async-done | bytes 1572896 | tf_op jit(solution)/shard_map/all_to_all | solution.py:405
  54.7 1.6 copy.25
  56.3 42.9 %shard_map.119 = f32[1,136,128]{2,1,0:T(8,128)} custom-call(s32[1]{0:T(128)} %bitcast.head_ref, bf16[2048,384]{1,0:T(8,128)(2,1)} %bitcast.16, f32[4,16,128]{2,1,0:T(8,128)} %mix_ref.1, f32[16,128]{1,0:T(8,128)} %fade_ref.1, f32[16,128,64]{2,1,0:T(8,128)} %copy.26.down_ref, f32[16,64,128]{2,1,0:T(8,128)} %up_ref.1, f32[16,128]{1,0:T(8,128)} %bonus_ref.1), custom_call_target="tpu_custom_call" | custom-call | tf_op jit(solution)/shard_map/pallas_call | solution.py:368
  99.2 0.0 all-gather.2.cloned.1.call-update
  99.2 58.0 %all-gather.2.cloned.1.call-done = f32[16,136,128]{2,1,0:T(8,128)} async-done(((f32[1,136,128]{2,1,0:T(8,128)}), f32[16,136,128]{2,1,0:T(8,128)}) %all-gather.2.cloned.1.call-update) | async-done | bytes 1114128 | tf_op jit(solution)/shard_map/all_gather | solution.py:416
  157.2 0.8 slice_bitcast_fusion.1
  158.0 0.6 copy.27
  158.7 2.3 %fusion.1 = (f32[16,64,128]{2,1,0:T(8,128)}, f32[16,128,64]{1,2,0:T(8,128)}) fusion(f32[16,136,128]{2,1,0:T(8,128)} %all-gather.2.cloned.1.call-done), kind=kLoop, calls=%fused_computation.4 | loop fusion | bytes 2097152 | tf_op jit(solution)/shard_map/slice | solution.py:417
  160.9 1.5 fusion
Async XLA Ops:
  12.1 8.5 %copy-start = (f32[16,128,64]{1,2,0:T(8,128)S(1)}, f32[16,128,64]{1,2,0:T(8,128)}, u32[]{:S(2)}) copy-start(f32[16,128,64]{1,2,0:T(8,128)} %param.13) | copy-start | bytes 1572868
  12.1 42.6 %all-to-all-start = ((bf16[128,16,384]{0,2,1:T(8,128)(2,1)}), bf16[128,16,384]{0,2,1:T(8,128)(2,1)S(1)}, u32[]{:S(2)}, u32[]{:S(2)}) async-start(bf16[128,16,384]{0,2,1:T(8,128)(2,1)} %bitcast.6), calls=%async_computation | async-start | bytes 3145728 | tf_op jit(solution)/shard_map/all_to_all | solution.py:405
  20.5 136.7 %all-gather.2.cloned.1.call-start = ((), (), s32[]{:S(2)}) async-start(), calls=%async_computation.1 | async-start | bytes 1183744 | tf_op jit(solution)/shard_map/all_gather | solution.py:416
Sparse Core Ops, SparseCore 0:
  99.4 57.7 all-gather.1
